TPU v7x, 512 devices: a whole 4x8x8 slice. The times are simulated.
512 devices in a mesh: row: 64 (over x, z, core), col: 8 (over y).
Axes of the slice: x: 4, y: 8, z: 8, core: 2. Of those that a mesh axis runs over, the one named last changes fastest.
Arguments:
- features: bfloat16 [262144, 512], P(('row', 'col')), may hold values from -6 to 6
- factor: float32 [262144, 1024], P(('row', 'col')), may hold values from -0.03 to 0.03
- ip_weights: float32 [262144], P(('row', 'col')), may hold values from 0.1 to 30
- pivot_owner: int32 [256], replicated, may hold values from 0 to 511, as said below
- pivot_position: int32 [256], replicated, may hold values from 0 to 511, as said below
Outputs:
- new_columns: float32 [262144, 256], P(('row', 'col'))
- gram_rows: float32 [256, 1280], replicated
Inputs may be any that keep to these rules, and one draw needn't show every extreme that they name: `pivot_owner`: each device owns at most 3 pivots, and some device owns exactly 3. `pivot_position`: pivots with the same owner have different positions.
All inputs are finite; a program needn't handle non-finite values.
Results may differ from a plain program's by a relative error of at most 0.0003.
Values may be sent and summed in bfloat16 or wider, within the bound.
A program may use at most 64 MiB of HBM per device.

v0:
```python
import jax
import jax.numpy as jnp
from jax import lax
from jax.sharding import Mesh
from jax.sharding import PartitionSpec as P

F = 512
ROW = ("row_0", "row_1", "row_2")
ROW_COL = ("row_0", "row_1", "row_2", "col")
kernel_rates = (0.25, 0.5, 1.0)
kernel_mixes = (0.5, 0.3, 0.2)


def copy_for_each(array, axis):
    copies = jnp.broadcast_to(array, (lax.axis_size(axis), *array.shape))
    return lax.all_to_all(copies, axis, split_axis=0, concat_axis=0, tiled=True)


def in_order(parts, dim):
    dims = list(parts.shape[1:])
    dims[dim] *= parts.shape[0]
    return jnp.moveaxis(parts, 0, dim).reshape(dims)


def gather_axes(array, axes, dim):
    far, near = axes
    parts = copy_for_each(copy_for_each(array, far), near)
    return in_order(parts.swapaxes(0, 1).reshape(-1, *array.shape), dim)


def cut_along(array, dim, length):
    before, after = (array.shape[:dim], array.shape[dim + 1 :])
    return jnp.moveaxis(array.reshape(*before, length, -1, *after), dim, 0)


def summed_on_arrival(array, axis, dim):
    parts = cut_along(array, dim, lax.axis_size(axis))
    arrived = lax.all_to_all(parts, axis, split_axis=0, concat_axis=0, tiled=True)
    return arrived.sum(axis=0)


def sum_by_axis(array, axes, dim):
    far, near = axes
    own = summed_on_arrival(cut_along(array, dim, lax.axis_size(far)), near, dim + 1)
    return jnp.sum(lax.all_to_all(own, far, 0, 0, tiled=True), axis=0)


def rows_for(lines, length):
    spare = -lines.shape[0] % length
    if not spare:
        return lines
    return jnp.concatenate([lines, jnp.zeros((spare, *lines.shape[1:]), lines.dtype)])


def total_of(array, axes):
    lines = array.reshape(-1)
    own = sum_by_axis(rows_for(lines, lax.axis_size(axes[0]) * lax.axis_size(axes[1])), axes, 0)
    whole = gather_axes(own, axes, 0)
    return whole[: len(lines)].reshape(array.shape)


def kernel_of(left, right):
    cross_term = jnp.dot(left, right.T, preferred_element_type=jnp.float32)
    left_norms = jnp.sum(jnp.square(left.astype(jnp.float32)), axis=1)
    right_norms = jnp.sum(jnp.square(right.astype(jnp.float32)), axis=1)
    distance = left_norms[:, None] + right_norms[None, :] - 2.0 * cross_term
    total = jnp.zeros_like(distance)
    for rate, mixing in zip(kernel_rates, kernel_mixes):
        total = total + mixing * jnp.exp(-(rate / F) * distance)
    return total


def body(features, factor, ip_weights, pivot_owner, pivot_position):
    devices = lax.axis_size(ROW) * lax.axis_size("col")
    device_rank = lax.axis_index(ROW) * lax.axis_size("col") + lax.axis_index("col")
    pivot_count = pivot_owner.shape[0]
    slot_count = 2 * pivot_count // devices + 2
    same_owner = pivot_owner[:, None] == pivot_owner[None, :]
    earlier = jnp.arange(pivot_count)[None, :] < jnp.arange(pivot_count)[:, None]
    slot_rank = jnp.sum((same_owner & earlier).astype(jnp.int32), axis=1)
    chosen = (pivot_owner == device_rank)[None, :] & (
        slot_rank[None, :] == jnp.arange(slot_count)[:, None]
    )
    filled = jnp.any(chosen, axis=1)[:, None]
    slot_rows = jnp.sum(jnp.where(chosen, pivot_position[None, :], 0), axis=1)
    slot_x = jnp.where(filled, features[slot_rows], jnp.zeros((), jnp.bfloat16))
    slot_h = jnp.where(filled, factor[slot_rows], 0.0)
    every_x = gather_axes(slot_x, (("row_0", "row_1"), ("row_2", "col")), 0)
    every_h = lax.all_gather(slot_h, ROW_COL, axis=0, tiled=True)
    source = pivot_owner * slot_count + slot_rank
    pivot_x = every_x[source]
    pivot_h = every_h[source]
    residual = kernel_of(features, pivot_x) - jnp.dot(
        factor, pivot_h.T, precision=lax.Precision.HIGHEST
    )
    block = kernel_of(pivot_x, pivot_x) - jnp.dot(
        pivot_h, pivot_h.T, precision=lax.Precision.HIGHEST
    )
    lower_block = jnp.linalg.cholesky(block)
    new_columns = jax.scipy.linalg.solve_triangular(lower_block, residual.T, lower=True).T
    weighted = new_columns * ip_weights[:, None]
    left_part = jnp.dot(weighted.T, factor, precision=lax.Precision.HIGHEST)
    right_part = jnp.dot(weighted.T, new_columns, precision=lax.Precision.HIGHEST)
    local_gram = jnp.concatenate([left_part, right_part], axis=1)
    summed = total_of(local_gram, (("row_0", "row_1"), ("row_2", "col")))
    total_samples = features.shape[0] * devices
    return (new_columns, summed / total_samples)


def solution(mesh):
    torus = Mesh(
        mesh.devices.reshape(4, 8, 2, mesh.shape["col"]), ("row_0", "row_1", "row_2", "col")
    )
    in_specs = (P(ROW_COL, None), P(ROW_COL, None), P(ROW_COL), P(), P())
    out_specs = (P(ROW_COL, None), P())
    return jax.shard_map(body, mesh=torus, in_specs=in_specs, out_specs=out_specs, check_vma=False)
```

profile of v0, /device:TPU:1, one launch (start us, length us, event | category | flops | bytes accessed | tf_op | source)
XLA Modules:
  0.0 362.9 jit_solution(6088916679859474437)
XLA Ops:
  7.2 1.0 convert_reduce_fusion
  8.2 0.7 broadcast_compare_fusion
  9.1 0.8 select_reduce_fusion.2
  9.9 0.6 gather_fusion.2
  10.4 0.7 select_bitcast_fusion.1
  11.2 1.7 gather_fusion
  13.0 22.7 %all_to_all.38 = bf16[32,3,512]{2,1,0:T(4,128)(2,1)S(1)} all-to-all(bf16[32,3,512]{2,1,0:T(4,128)(2,1)S(1)} %broadcast_in_dim.74), channel_id=1, replica_groups=mesh['row_0'=4,'row_1'=8,'row_2'=2,'col'=8] {'row_0','row_1'}, dimensions={0} | all-to-all | bytes 196608 | tf_op jit(solution)/shard_map/all_to_all | solution.py:16
  35.6 1.4 broadcast_in_dim.75
  37.1 9.3 %all-to-all-start.1 = ((bf16[16,32,3,512]{3,1,2,0:T(8,128)(2,1)}), bf16[16,32,3,512]{3,1,2,0:T(8,128)(2,1)}, u32[]{:S(2)}, u32[]{:S(2)}) async-start(bf16[16,32,3,512]{3,1,2,0:T(8,128)(2,1)} %broadcast_in_dim.75), calls=%async_computation.1 | async-start | bytes 3145728 | tf_op jit(solution)/shard_map/all_to_all | solution.py:16
  46.6 37.9 %all-to-all-done.1 = bf16[16,32,3,512]{3,1,2,0:T(8,128)(2,1)} async-done(((bf16[16,32,3,512]{3,1,2,0:T(8,128)(2,1)}), bf16[16,32,3,512]{3,1,2,0:T(8,128)(2,1)}, u32[]{:S(2)}, u32[]{:S(2)}) %all-to-all-start.1) | async-done | bytes 1572896 | tf_op jit(solution)/shard_map/all_to_all | solution.py:16
  84.5 4.2 %copy.42 = bf16[32,16,3,512]{3,2,1,0:T(4,128)(2,1)} copy(bf16[32,16,3,512]{3,0,2,1:T(8,128)(2,1)} %bitcast.2) | data formatting | bytes 3145728 | tf_op jit(solution)/shard_map/transpose | solution.py:28
  88.6 5.1 %reshape_reshape.3 = bf16[1536,512]{1,0:T(8,128)(2,1)} reshape(bf16[32,16,3,512]{3,2,1,0:T(4,128)(2,1)} %copy.42) | data formatting | bytes 3145728 | tf_op jit(solution)/shard_map/reshape;reshape | solution.py:22
  93.7 2.8 gather_fusion.1
  96.8 0.8 copy.44
  97.8 1.1 fusion
  98.9 55.2 %all-gather.3.cloned.1.call-done = f32[512,3,1024]{2,1,0:T(4,128)} async-done(((f32[1,3,1024]{2,1,0:T(4,128)}), f32[512,3,1024]{2,1,0:T(4,128)}) %all-gather.3.cloned.1.call-update) | async-done | bytes 6291472 | tf_op jit(solution)/shard_map/all_gather | solution.py:89
  154.1 10.8 %reshape.108 = f32[1536,1024]{1,0:T(8,128)} reshape(f32[512,3,1024]{2,1,0:T(4,128)} %all-gather.3.cloned.1.call-done) | data formatting | bytes 12582912
  164.9 4.4 %gather_fusion.3 = f32[256,1024]{1,0:T(8,128)S(1)} fusion(f32[1536,1024]{1,0:T(8,128)} %reshape.108, s32[1024]{0:T(1024)S(1)} %pad_clamp_fusion), kind=kCustom, calls=%fused_computation.3 | custom fusion | bytes 2098176 | tf_op jit(solution)/shard_map/gather | solution.py:92
  169.3 1.7 fusion.26
  171.0 2.9 convolution_subtract_fusion
  173.9 1.1 copy.45
  174.9 1.4 fusion.9
  176.4 11.7 %cholesky.50 = f32[128,128]{1,0:T(8,128)S(1)} custom-call(f32[128,128]{1,0:T(8,128)S(1)} %cholesky.118), custom_call_target="Cholesky" | custom-call | tf_op jit(solution)/shard_map/jit(cholesky)/cholesky | solution.py:99
  188.2 9.8 %custom-call.15 = f32[1,128,128]{1,2,0:T(8,128)S(1)} custom-call(f32[1,128,128]{2,1,0:T(8,128)S(1)} %get-tuple-element.35), custom_call_target="InvertDiagBlocksLowerTriangular" | custom-call | tf_op jit(solution)/shard_map/jit(cholesky)/cholesky | solution.py:99
  198.4 11.9 %cholesky.105 = f32[128,128]{1,0:T(8,128)S(1)} custom-call(f32[128,128]{1,0:T(8,128)S(1)} %convolution_subtract_fusion.2), custom_call_target="Cholesky" | custom-call | tf_op jit(solution)/shard_map/jit(cholesky)/cholesky | solution.py:99
  210.4 0.7 compare_reduce_fusion
  212.6 4.1 %while.1 = (s32[]{:T(128)}, f32[256,256]{1,0:T(8,128)S(1)}, s32[2,2]{1,0:T(2,128)S(1)}, f32[2,128,128]{2,1,0:T(8,128)S(1)}, s32[]{:T(128)}) while((s32[]{:T(128)}, f32[256,256]{1,0:T(8,128)S(1)}, s32[2,2]{1,0:T(2,128)S(1)}, f32[2,128,128]{2,1,0:T(8,128)S(1)}, s32[]{:T(128)}) %tuple.33), condition=%wide.while_cond, body=%wide.while_body.sunk | while | flops 2 | bytes 131189 | solution.py:100
  212.6 0.6 fusion.41
  213.2 1.4 bitcast_dynamic-update-slice_fusion.2
  214.6 0.6 fusion.41
  215.2 1.4 bitcast_dynamic-update-slice_fusion.2
  216.7 19.7 %custom-call.16 = f32[2,128,128]{1,2,0:T(8,128)S(1)} custom-call(f32[2,128,128]{2,1,0:T(8,128)S(1)} %get-tuple-element.9), custom_call_target="InvertDiagBlocksLowerTriangular" | custom-call | tf_op jit(solution)/shard_map/jit(_solve_triangular)/triangular_solve | solution.py:100
  237.6 0.6 fusion.1
  238.2 1.9 fusion.3
  240.1 1.2 pad_maximum_fusion
  241.3 2.5 reshape_reshape_reshape.4
  243.8 1.7 copy.55
  245.5 37.5 %all_to_all.39 = f32[16,32,640]{2,1,0:T(8,128)} all-to-all(f32[16,32,640]{2,1,0:T(8,128)S(1)} %bitcast.69), channel_id=1, replica_groups=mesh['row_0'=4,'row_1'=8,'row_2'=2,'col'=8] {'row_2','col'}, dimensions={0} | all-to-all | bytes 2621440 | tf_op jit(solution)/shard_map/all_to_all | solution.py:38
  283.0 1.4 reduce_sum.69
  284.5 14.5 %all_to_all.40 = f32[32,1,640]{2,1,0:T(1,128)S(1)} all-to-all(f32[32,1,640]{2,1,0:T(1,128)S(1)} %all_to_all.27), channel_id=1, replica_groups=mesh['row_0'=4,'row_1'=8,'row_2'=2,'col'=8] {'row_0','row_1'}, dimensions={0} | all-to-all | bytes 163840 | tf_op jit(solution)/shard_map/all_to_all | solution.py:45
  299.1 12.3 %all_to_all.41 = f32[32,1,640]{2,1,0:T(1,128)S(1)} all-to-all(f32[32,1,640]{2,1,0:T(1,128)S(1)} %broadcast_in_dim.79), channel_id=1, replica_groups=mesh['row_0'=4,'row_1'=8,'row_2'=2,'col'=8] {'row_0','row_1'}, dimensions={0} | all-to-all | bytes 163840 | tf_op jit(solution)/shard_map/all_to_all | solution.py:16
  311.4 1.2 broadcast_in_dim.80
  312.6 7.8 %all-to-all-start.5 = ((f32[16,32,640]{2,1,0:T(8,128)}), f32[16,32,640]{2,1,0:T(8,128)}, u32[]{:S(2)}, u32[]{:S(2)}) async-start(f32[16,32,640]{2,1,0:T(8,128)} %broadcast_in_dim.80), calls=%async_computation.5 | async-start | bytes 2621440 | tf_op jit(solution)/shard_map/all_to_all | solution.py:16
  320.4 1.0 copy.49
  321.4 31.0 %all-to-all-done.5 = f32[16,32,640]{2,1,0:T(8,128)} async-done(((f32[16,32,640]{2,1,0:T(8,128)}), f32[16,32,640]{2,1,0:T(8,128)}, u32[]{:S(2)}, u32[]{:S(2)}) %all-to-all-start.5) | async-done | bytes 1310752 | tf_op jit(solution)/shard_map/all_to_all | solution.py:16
  352.4 1.4 multiply_bitcast_fusion
  353.8 0.8 copy.48
  354.6 1.4 div.20
  (45 shorter events, 3.1 us)
Async XLA Ops:
  7.2 2.7 copy-start
  7.2 147.0 %all-gather.3.cloned.1.call-start = ((), (), s32[]{:S(2)}) async-start(), calls=%async_computation.6 | async-start | bytes 8404992 | tf_op jit(solution)/shard_map/all_gather | solution.py:89
  37.1 9.3 %copy-start.4 = (s32[256]{0:T(256)S(1)}, s32[256]{0:T(256)}, u32[]{:S(2)}) copy-start(s32[256]{0:T(256)} %param.8) | copy-start | bytes 3076
  37.1 9.4 %copy-start.1 = (bf16[512,512]{1,0:T(8,128)(2,1)S(1)}, bf16[512,512]{1,0:T(8,128)(2,1)}, u32[]{:S(2)}) copy-start(bf16[512,512]{1,0:T(8,128)(2,1)} %param.5) | copy-start | bytes 1572868
  37.1 47.4 %all-to-all-start.1 = ((bf16[16,32,3,512]{3,1,2,0:T(8,128)(2,1)}), bf16[16,32,3,512]{3,1,2,0:T(8,128)(2,1)}, u32[]{:S(2)}, u32[]{:S(2)}) async-start(bf16[16,32,3,512]{3,1,2,0:T(8,128)(2,1)} %broadcast_in_dim.75), calls=%async_computation.1 | async-start | bytes 3145728 | tf_op jit(solution)/shard_map/all_to_all | solution.py:16
  169.3 1.7 copy-start.3
  176.4 60.0 %copy-start.2 = (f32[256,512]{1,0:T(8,128)S(1)}, f32[256,512]{1,0:T(8,128)}, u32[]{:S(2)}) copy-start(f32[256,512]{1,0:T(8,128)} %convolution_subtract_fusion) | copy-start | bytes 1572868
  212.5 25.1 %copy-start.5 = (f32[512]{0:T(512)S(1)}, f32[512]{0:T(512)}, u32[]{:S(2)}) copy-start(f32[512]{0:T(512)} %param.7) | copy-start | bytes 6148
  312.6 39.8 %all-to-all-start.5 = ((f32[16,32,640]{2,1,0:T(8,128)}), f32[16,32,640]{2,1,0:T(8,128)}, u32[]{:S(2)}, u32[]{:S(2)}) async-start(f32[16,32,640]{2,1,0:T(8,128)} %broadcast_in_dim.80), calls=%async_computation.5 | async-start | bytes 2621440 | tf_op jit(solution)/shard_map/all_to_all | solution.py:16
Sparse Core Ops, SparseCore 0:
  13.0 141.0 all-gather.2
where the time goes:
time: 364 us; the launch traced here: 363 us
  waiting for transfers between devices  124 us (34%)
  blocking collectives  86.9 us (24%)
  other arithmetic  63.1 us (17%)
  local copies, waits for them, and re-layouts  45.7 us (13%)
  starting transfers between devices  17.2 us (5%)
  between operations  15.7 us (4%)
  matrix products  10.2 us (3%)
    all_to_all x2, waiting for transfers between devices, copy_for_each(): return lax.all_to_all(copies, axis, split_axis=0, concat_axis=0, tiled=True)  68.9 us
    all_gather x1, waiting for transfers between devices, body(): every_h = lax.all_gather(slot_h, ROW_COL, axis=0, tiled=True)  55.2 us
    all_to_all x1, blocking collectives, summed_on_arrival(): lax.all_to_all(parts, axis, split_axis=0, concat_axis=0, tiled=True)  37.5 us
    all_to_all x2, blocking collectives, copy_for_each(): return lax.all_to_all(copies, axis, split_axis=0, concat_axis=0, tiled=True)  34.9 us
    another operation x6, other arithmetic, body(): lower_block = jnp.linalg.cholesky(block)  34.2 us
    another operation x3, other arithmetic, body(): jax.scipy.linalg.solve_triangular(lower_block, residual.T, lower=True)  19.7 us
    all_to_all x2, starting transfers between devices, copy_for_each(): return lax.all_to_all(copies, axis, split_axis=0, concat_axis=0, tiled=True)  17.1 us
    all_to_all x1, blocking collectives, sum_by_axis(): return jnp.sum(lax.all_to_all(own, far, 0, 0, tiled=True), axis=0)  14.5 us
  transfers between devices with their start and end apart: 3, of which 3 were waited for; matrix products, arithmetic and copies ran while one was open for 5% of the time, Pallas kernels for 0%

commit v1 on v0

--- a/solution.py
+++ b/solution.py
@@ -86,7 +86,15 @@
     slot_x = jnp.where(filled, features[slot_rows], jnp.zeros((), jnp.bfloat16))
     slot_h = jnp.where(filled, factor[slot_rows], 0.0)
     every_x = gather_axes(slot_x, (("row_0", "row_1"), ("row_2", "col")), 0)
-    every_h = lax.all_gather(slot_h, ROW_COL, axis=0, tiled=True)
+    every_h = jnp.concatenate(
+        jax.lax.all_to_all(
+            jnp.stack([slot_h] * jax.lax.axis_size(ROW_COL), 0),
+            ROW_COL,
+            split_axis=0,
+            concat_axis=0,
+        ),
+        0,
+    )
     source = pivot_owner * slot_count + slot_rank
     pivot_x = every_x[source]
     pivot_h = every_h[source]

time: 364 us -> 483 us (1.33)
  waiting for transfers between devices: 124 us -> 240 us
  between operations: 15.7 us -> 2.28 us
  starting transfers between devices: 17.2 us -> 28.3 us
  local copies, waits for them, and re-layouts: 45.7 us -> 50.9 us
    all_to_all x0 -> x1, waiting for transfers between devices: none -> 171 us  [body(): jax.lax.all_to_all(jnp.stack([slot_h] * jax.lax.axis_size(ROW_COL), 0), R...]
    all_gather x1 -> x0, waiting for transfers between devices: 55.2 us -> none  [body(): every_h = lax.all_gather(slot_h, ROW_COL, axis=0, tiled=True)]
    all_to_all x0 -> x1, starting transfers between devices: none -> 11.3 us  [body(): jax.lax.all_to_all(jnp.stack([slot_h] * jax.lax.axis_size(ROW_COL), 0), R...]
    reshape x0 -> x1, local copies, waits for them, and re-layouts: none -> 10.8 us  [body(): jnp.concatenate(jax.lax.all_to_all(jnp.stack([slot_h] * jax.lax.axis_size...]
    unnamed x15 -> x14, local copies, waits for them, and re-layouts: 11.8 us -> 1.04 us
    another operation x6 -> x7, local copies, waits for them, and re-layouts: 4.06 us -> 9.41 us  [the longest x1 5.35 us: body(): jnp.stack([slot_h] * jax.lax.axis_size(ROW_COL), 0)]
  transfers between devices with their start and end apart: 3 -> 3, of which waited for: 3 -> 3; matrix products, arithmetic and copies ran while one was open for 5% -> 3% of each run, Pallas kernels for 0% -> 0%
where the time goes in v1:
time: 483 us; the launch traced here: 481 us
  waiting for transfers between devices  240 us (50%)
  blocking collectives  87.4 us (18%)
  other arithmetic  62.5 us (13%)
  local copies, waits for them, and re-layouts  50.9 us (11%)
  starting transfers between devices  28.3 us (6%)
  matrix products  10.2 us (2%)
    all_to_all x1, waiting for transfers between devices, body(): jax.lax.all_to_all(jnp.stack([slot_h] * jax.lax.axis_size(ROW_COL), 0), R...  171 us
    all_to_all x2, waiting for transfers between devices, copy_for_each(): return lax.all_to_all(copies, axis, split_axis=0, concat_axis=0, tiled=True)  68.4 us
    all_to_all x1, blocking collectives, summed_on_arrival(): lax.all_to_all(parts, axis, split_axis=0, concat_axis=0, tiled=True)  38.3 us
    all_to_all x2, blocking collectives, copy_for_each(): return lax.all_to_all(copies, axis, split_axis=0, concat_axis=0, tiled=True)  34.9 us
    another operation x6, other arithmetic, body(): lower_block = jnp.linalg.cholesky(block)  34.2 us
    another operation x3, other arithmetic, body(): jax.scipy.linalg.solve_triangular(lower_block, residual.T, lower=True)  19.7 us
    all_to_all x2, starting transfers between devices, copy_for_each(): return lax.all_to_all(copies, axis, split_axis=0, concat_axis=0, tiled=True)  17 us
    all_to_all x1, blocking collectives, sum_by_axis(): return jnp.sum(lax.all_to_all(own, far, 0, 0, tiled=True), axis=0)  14.1 us
  transfers between devices with their start and end apart: 3, of which 3 were waited for; matrix products, arithmetic and copies ran while one was open for 3% of the time, Pallas kernels for 0%

profile of v1, /device:TPU:1, one launch (start us, length us, event | category | flops | bytes accessed | tf_op | source)
XLA Modules:
  0.0 481.3 jit_solution(16684951249152839889)
XLA Ops:
  0.6 1.0 convert_reduce_fusion
  1.7 0.7 broadcast_compare_fusion
  2.5 0.8 select_reduce_fusion.2
  3.3 1.7 gather_fusion
  5.1 22.7 %all_to_all.43 = bf16[32,3,512]{2,1,0:T(4,128)(2,1)S(1)} all-to-all(bf16[32,3,512]{2,1,0:T(4,128)(2,1)S(1)} %broadcast_in_dim.74), channel_id=1, replica_groups=mesh['row_0'=4,'row_1'=8,'row_2'=2,'col'=8] {'row_0','row_1'}, dimensions={0} | all-to-all | bytes 196608 | tf_op jit(solution)/shard_map/all_to_all | solution.py:16
  27.8 1.3 broadcast_in_dim.75
  29.1 9.2 %all-to-all-start.1 = ((bf16[16,32,3,512]{3,1,2,0:T(8,128)(2,1)}), bf16[16,32,3,512]{3,1,2,0:T(8,128)(2,1)}, u32[]{:S(2)}, u32[]{:S(2)}) async-start(bf16[16,32,3,512]{3,1,2,0:T(8,128)(2,1)} %broadcast_in_dim.75), calls=%async_computation.1 | async-start | bytes 3145728 | tf_op jit(solution)/shard_map/all_to_all | solution.py:16
  39.0 37.4 %all-to-all-done.1 = bf16[16,32,3,512]{3,1,2,0:T(8,128)(2,1)} async-done(((bf16[16,32,3,512]{3,1,2,0:T(8,128)(2,1)}), bf16[16,32,3,512]{3,1,2,0:T(8,128)(2,1)}, u32[]{:S(2)}, u32[]{:S(2)}) %all-to-all-start.1) | async-done | bytes 1572896 | tf_op jit(solution)/shard_map/all_to_all | solution.py:16
  76.4 5.3 %stack.2 = f32[512,3,1024]{2,1,0:T(4,128)} broadcast(f32[3,1024]{1,0:T(4,128)S(1)} %broadcast_select_fusion), dimensions={1,2} | broadcast | bytes 6303744 | tf_op jit(solution)/shard_map/stack | solution.py:91
  81.8 11.3 %all-to-all-start.2 = ((f32[512,3,1024]{2,1,0:T(4,128)}), f32[512,3,1024]{2,1,0:T(4,128)}, u32[]{:S(2)}, u32[]{:S(2)}) async-start(f32[512,3,1024]{2,1,0:T(4,128)} %stack.2), calls=%async_computation.2 | async-start | bytes 16777216 | tf_op jit(solution)/shard_map/all_to_all | solution.py:90
  93.3 4.1 copy.42
  97.4 5.0 %reshape_reshape.3 = bf16[1536,512]{1,0:T(8,128)(2,1)} reshape(bf16[32,16,3,512]{3,2,1,0:T(4,128)(2,1)} %copy.42) | data formatting | bytes 3145728 | tf_op jit(solution)/shard_map/reshape;reshape | solution.py:22
  102.5 2.8 gather_fusion.1
  105.6 0.8 copy.44
  106.5 1.1 fusion
  107.7 171.3 %all-to-all-done.2 = f32[512,3,1024]{2,1,0:T(4,128)} async-done(((f32[512,3,1024]{2,1,0:T(4,128)}), f32[512,3,1024]{2,1,0:T(4,128)}, u32[]{:S(2)}, u32[]{:S(2)}) %all-to-all-start.2) | async-done | bytes 6291488 | tf_op jit(solution)/shard_map/all_to_all | solution.py:90
  279.0 10.8 %reshape.64 = f32[1536,1024]{1,0:T(8,128)} reshape(f32[512,3,1024]{2,1,0:T(4,128)} %all-to-all-done.2) | data formatting | bytes 12582912 | tf_op jit(solution)/shard_map/reshape | solution.py:89
  289.7 4.4 gather_fusion.3
  294.1 1.7 fusion.26
  295.8 2.9 convolution_subtract_fusion
  298.7 1.1 copy.45
  299.8 1.4 fusion.9
  301.2 11.7 %cholesky.50 = f32[128,128]{1,0:T(8,128)S(1)} custom-call(f32[128,128]{1,0:T(8,128)S(1)} %cholesky.118), custom_call_target="Cholesky" | custom-call | tf_op jit(solution)/shard_map/jit(cholesky)/cholesky | solution.py:107
  313.0 9.8 %custom-call.15 = f32[1,128,128]{1,2,0:T(8,128)S(1)} custom-call(f32[1,128,128]{2,1,0:T(8,128)S(1)} %get-tuple-element.35), custom_call_target="InvertDiagBlocksLowerTriangular" | custom-call | tf_op jit(solution)/shard_map/jit(cholesky)/cholesky | solution.py:107
  323.3 11.9 %cholesky.105 = f32[128,128]{1,0:T(8,128)S(1)} custom-call(f32[128,128]{1,0:T(8,128)S(1)} %convolution_subtract_fusion.2), custom_call_target="Cholesky" | custom-call | tf_op jit(solution)/shard_map/jit(cholesky)/cholesky | solution.py:107
  335.2 0.7 compare_reduce_fusion
  337.4 4.1 while.1
  337.4 0.6 fusion.41
  338.0 1.4 bitcast_dynamic-update-slice_fusion.2
  339.5 0.6 fusion.41
  340.1 1.4 bitcast_dynamic-update-slice_fusion.2
  341.5 19.7 %custom-call.16 = f32[2,128,128]{1,2,0:T(8,128)S(1)} custom-call(f32[2,128,128]{2,1,0:T(8,128)S(1)} %get-tuple-element.9), custom_call_target="InvertDiagBlocksLowerTriangular" | custom-call | tf_op jit(solution)/shard_map/jit(_solve_triangular)/triangular_solve | solution.py:108
  362.4 0.6 fusion.1
  363.1 1.9 fusion.3
  365.0 1.2 pad_maximum_fusion
  366.1 2.5 reshape_reshape_reshape.4
  368.6 1.7 copy.55
  370.4 38.3 %all_to_all.44 = f32[16,32,640]{2,1,0:T(8,128)} all-to-all(f32[16,32,640]{2,1,0:T(8,128)S(1)} %bitcast.67), channel_id=1, replica_groups=mesh['row_0'=4,'row_1'=8,'row_2'=2,'col'=8] {'row_2','col'}, dimensions={0} | all-to-all | bytes 2621440 | tf_op jit(solution)/shard_map/all_to_all | solution.py:38
  408.7 1.4 reduce_sum.69
  410.2 14.1 %all_to_all.45 = f32[32,1,640]{2,1,0:T(1,128)S(1)} all-to-all(f32[32,1,640]{2,1,0:T(1,128)S(1)} %all_to_all.31), channel_id=1, replica_groups=mesh['row_0'=4,'row_1'=8,'row_2'=2,'col'=8] {'row_0','row_1'}, dimensions={0} | all-to-all | bytes 163840 | tf_op jit(solution)/shard_map/all_to_all | solution.py:45
  424.4 12.3 %all_to_all.46 = f32[32,1,640]{2,1,0:T(1,128)S(1)} all-to-all(f32[32,1,640]{2,1,0:T(1,128)S(1)} %broadcast_in_dim.79), channel_id=1, replica_groups=mesh['row_0'=4,'row_1'=8,'row_2'=2,'col'=8] {'row_0','row_1'}, dimensions={0} | all-to-all | bytes 163840 | tf_op jit(solution)/shard_map/all_to_all | solution.py:16
  436.7 1.2 broadcast_in_dim.80
  437.8 7.8 %all-to-all-start.6 = ((f32[16,32,640]{2,1,0:T(8,128)}), f32[16,32,640]{2,1,0:T(8,128)}, u32[]{:S(2)}, u32[]{:S(2)}) async-start(f32[16,32,640]{2,1,0:T(8,128)} %broadcast_in_dim.80), calls=%async_computation.6 | async-start | bytes 2621440 | tf_op jit(solution)/shard_map/all_to_all | solution.py:16
  445.7 1.0 copy.49
  446.7 31.0 %all-to-all-done.6 = f32[16,32,640]{2,1,0:T(8,128)} async-done(((f32[16,32,640]{2,1,0:T(8,128)}), f32[16,32,640]{2,1,0:T(8,128)}, u32[]{:S(2)}, u32[]{:S(2)}) %all-to-all-start.6) | async-done | bytes 1310752 | tf_op jit(solution)/shard_map/all_to_all | solution.py:16
  477.7 1.4 multiply_bitcast_fusion
  479.1 0.8 copy.48
  479.9 1.4 div.20
  (45 shorter events, 3.6 us)
Async XLA Ops:
  0.6 37.7 %copy-start = (f32[512,1024]{1,0:T(8,128)S(1)}, f32[512,1024]{1,0:T(8,128)}, u32[]{:S(2)}) copy-start(f32[512,1024]{1,0:T(8,128)} %param.6) | copy-start | bytes 6291460
  29.1 47.3 %all-to-all-start.1 = ((bf16[16,32,3,512]{3,1,2,0:T(8,128)(2,1)}), bf16[16,32,3,512]{3,1,2,0:T(8,128)(2,1)}, u32[]{:S(2)}, u32[]{:S(2)}) async-start(bf16[16,32,3,512]{3,1,2,0:T(8,128)(2,1)} %broadcast_in_dim.75), calls=%async_computation.1 | async-start | bytes 3145728 | tf_op jit(solution)/shard_map/all_to_all | solution.py:16
  81.8 11.3 %copy-start.4 = (s32[256]{0:T(256)S(1)}, s32[256]{0:T(256)}, u32[]{:S(2)}) copy-start(s32[256]{0:T(256)} %param.8) | copy-start | bytes 3076
  81.8 11.4 %copy-start.1 = (bf16[512,512]{1,0:T(8,128)(2,1)S(1)}, bf16[512,512]{1,0:T(8,128)(2,1)}, u32[]{:S(2)}) copy-start(bf16[512,512]{1,0:T(8,128)(2,1)} %param.5) | copy-start | bytes 1572868
  81.8 197.2 %all-to-all-start.2 = ((f32[512,3,1024]{2,1,0:T(4,128)}), f32[512,3,1024]{2,1,0:T(4,128)}, u32[]{:S(2)}, u32[]{:S(2)}) async-start(f32[512,3,1024]{2,1,0:T(4,128)} %stack.2), calls=%async_computation.2 | async-start | bytes 16777216 | tf_op jit(solution)/shard_map/all_to_all | solution.py:90
  294.1 1.7 copy-start.3
  301.2 60.0 %copy-start.2 = (f32[256,512]{1,0:T(8,128)S(1)}, f32[256,512]{1,0:T(8,128)}, u32[]{:S(2)}) copy-start(f32[256,512]{1,0:T(8,128)} %convolution_subtract_fusion) | copy-start | bytes 1572868
  337.3 25.1 %copy-start.5 = (f32[512]{0:T(512)S(1)}, f32[512]{0:T(512)}, u32[]{:S(2)}) copy-start(f32[512]{0:T(512)} %param.7) | copy-start | bytes 6148
  437.8 39.8 %all-to-all-start.6 = ((f32[16,32,640]{2,1,0:T(8,128)}), f32[16,32,640]{2,1,0:T(8,128)}, u32[]{:S(2)}, u32[]{:S(2)}) async-start(f32[16,32,640]{2,1,0:T(8,128)} %broadcast_in_dim.80), calls=%async_computation.6 | async-start | bytes 2621440 | tf_op jit(solution)/shard_map/all_to_all | solution.py:16
